TPU v7x, 512 devices: a whole 4x4x16 slice. The times are simulated.
512 devices in a mesh: seq: 32 (over x, y, core), key: 16 (over z).
Axes of the slice: x: 4, y: 4, z: 16, core: 2. Of those that a mesh axis runs over, the one named last changes fastest.
Arguments:
- query_rows: bfloat16 [8192, 16, 256], P('seq', None, 'key'), may hold values from -0.375 to 0.375
- key_rows: bfloat16 [8192, 16, 256], P('seq', None, 'key'), may hold values from -0.1875 to 0.1875
- value_rows: bfloat16 [8192, 16, 256], P('seq', 'key'), may hold values from -6 to 6
- out_grad: bfloat16 [8192, 16, 256], P('seq', 'key')
- log_gates: float32 [16, 8192], P('key', 'seq'), may hold values from -0.8 to 0, as said below
- write_rate: float32 [16, 8192], P('key', 'seq'), may hold values from 0.1 to 0.8
- group_inverse: bfloat16 [64, 16, 128, 128], P('seq', 'key'), as said below
- states: bfloat16 [64, 16, 256, 256], P('seq', None, 'key'), may hold values from -0.75 to 0.75
Outputs:
- grad_query: bfloat16 [8192, 16, 256], P('seq', None, 'key')
- grad_key: bfloat16 [8192, 16, 256], P('seq', None, 'key')
- grad_value: bfloat16 [8192, 16, 256], P('seq', 'key')
- grad_square: float32 [], replicated
Inputs may be any that keep to these rules, and one draw needn't show every extreme that they name: `group_inverse`: each group's matrix is unit lower triangular: ones on the diagonal, zeros above it. `log_gates`: every entry is the logarithm of a decay factor, never positive.
All inputs are finite; a program needn't handle non-finite values.
Results may differ from a plain program's by a relative error of at most 0.007.
Values may be sent and summed in bfloat16 or wider, within the bound.
No kernel may reach another device: no remote copies, remote signals or barrier semaphores. Data moves between devices by JAX's collectives and lax.ppermute only.
A program may use at most 128 MiB of HBM per device.

v0:
```python
import jax
import jax.numpy as jnp
from jax import lax
from jax.sharding import PartitionSpec as P

highest_mode = lax.Precision.HIGHEST


def from_behind(value, axis, steps):
    count = lax.axis_size(axis)
    first, last = (max(0, -steps), min(count, count - steps))
    return lax.ppermute(value, axis, [(source, source + steps) for source in range(first, last)])


def mixed_dot(form, left, right):
    return jnp.einsum(form, left, right, preferred_element_type=jnp.float32)


def precise_product(form, left, right):
    return jnp.einsum(form, left.astype(jnp.float32), right, precision=highest_mode)


def linear_part(state_in, write_block, key_block, decay_block):
    through = precise_product("thk,hkm->thm", key_block, state_in)
    return decay_block[:, None, None] * state_in - precise_product(
        "thk,thm->hkm", write_block, through
    )


def device_map(state_out, written_keys, key_result, end_decay, offset_term):

    def group_step(state_in, pieces):
        write_block, key_block, decay_block, offset_block = pieces
        return (linear_part(state_in, write_block, key_block, decay_block) + offset_block, state_in)

    return lax.scan(
        group_step, state_out, (written_keys, key_result, end_decay, offset_term), reverse=True
    )


def token_wise(factor):
    return jnp.transpose(factor, (0, 2, 1))[:, :, :, None]


def square_sum(array):
    return jnp.sum(jnp.square(array.astype(jnp.float32)))


def local(query_rows, key_rows, value_rows, out_grad, log_gates, write_rate, group_inverse, states):
    halfway_point = jnp.bfloat16
    query_heads, key_heads, state_heads = (
        lax.all_to_all(query_rows, "key", split_axis=1, concat_axis=2, tiled=True),
        lax.all_to_all(key_rows, "key", split_axis=1, concat_axis=2, tiled=True),
        lax.all_to_all(states, "key", split_axis=1, concat_axis=2, tiled=True),
    )
    group_count, head_local, group_len, _ = group_inverse.shape
    token_count, _, key_width = query_heads.shape
    value_width = value_rows.shape[2]
    query_blk = query_heads.reshape(group_count, group_len, head_local, key_width)
    key_blk = key_heads.reshape(group_count, group_len, head_local, key_width)
    value_blk = value_rows.reshape(group_count, group_len, head_local, value_width)
    grad_blk = out_grad.reshape(group_count, group_len, head_local, value_width)
    gate_blk = jnp.transpose(log_gates.reshape(head_local, group_count, group_len), (1, 0, 2))
    rate_blk = jnp.transpose(write_rate.reshape(head_local, group_count, group_len), (1, 0, 2))
    gamma = jnp.cumsum(gate_blk, axis=2)
    final_gamma_value = gamma[:, :, -1:]
    incoming_decay = jnp.exp(gamma)
    outgoing_decay = jnp.exp(final_gamma_value - gamma)
    row_ids = lax.broadcasted_iota(jnp.int32, (group_len, group_len), 0)
    col_ids = lax.broadcasted_iota(jnp.int32, (group_len, group_len), 1)
    lower = row_ids >= col_ids
    spread = gamma[:, :, :, None] - gamma[:, :, None, :]
    decay_mask = jnp.where(lower, jnp.exp(jnp.where(lower, spread, 0.0)), 0.0)
    key_scaled = (key_blk * token_wise(rate_blk * incoming_decay)).astype(halfway_point)
    written_keys = mixed_dot("nhts,nshk->nthk", group_inverse, key_scaled).astype(halfway_point)
    scaled_values = (value_blk * token_wise(rate_blk)).astype(halfway_point)
    fresh_values = (
        mixed_dot("nhts,nshv->nthv", group_inverse, scaled_values)
        - mixed_dot("nthk,nhkv->nthv", written_keys, state_heads)
    ).astype(halfway_point)
    score_mat = (mixed_dot("nthk,nshk->nhts", query_blk, key_blk) * decay_mask).astype(
        halfway_point
    )
    key_result = (key_blk * token_wise(outgoing_decay)).astype(halfway_point)
    incoming_query = (query_blk * token_wise(incoming_decay)).astype(halfway_point)
    inner_gradient = mixed_dot("nhts,nthv->nshv", score_mat, grad_blk)
    offset_term = mixed_dot("nthk,nthv->nhkv", incoming_query, grad_blk) - precise_product(
        "nthk,nthv->nhkv", written_keys, inner_gradient
    )
    end_decay = jnp.exp(final_gamma_value[:, :, 0])
    empty_state = jnp.zeros((head_local, key_width, value_width), jnp.float32)

    def relay_hop(hop_index, incoming):
        state_in, _ = device_map(incoming, written_keys, key_result, end_decay, offset_term)
        return from_behind(state_in, "seq", -1)

    state_out = lax.fori_loop(0, lax.axis_size("seq") - 1, relay_hop, empty_state)
    _, state_gradient = device_map(state_out, written_keys, key_result, end_decay, offset_term)
    value_rounding = (
        inner_gradient + precise_product("nthk,nhkv->nthv", key_result, state_gradient)
    ).astype(halfway_point)
    value_grad_blk = (
        token_wise(rate_blk) * mixed_dot("nhts,nthv->nshv", group_inverse, value_rounding)
    ).astype(halfway_point)
    score_gradient = (mixed_dot("nthv,nshv->nhts", grad_blk, fresh_values) * decay_mask).astype(
        halfway_point
    )
    write_gradient = (-mixed_dot("nthv,nhkv->nthk", value_rounding, state_heads)).astype(
        halfway_point
    )
    state_rounding = state_gradient.astype(halfway_point)
    query_grad_blk = (
        token_wise(incoming_decay) * mixed_dot("nthv,nhkv->nthk", grad_blk, state_heads)
        + mixed_dot("nhts,nshk->nthk", score_gradient, key_blk)
    ).astype(halfway_point)
    key_grad_blk = (
        mixed_dot("nhts,nthk->nshk", score_gradient, query_blk)
        + token_wise(outgoing_decay) * mixed_dot("nthv,nhkv->nthk", fresh_values, state_rounding)
        + token_wise(rate_blk * incoming_decay)
        * mixed_dot("nhts,nthk->nshk", group_inverse, write_gradient)
    ).astype(halfway_point)
    query_grad_heads = query_grad_blk.reshape(token_count, head_local, key_width)
    key_grad_heads = key_grad_blk.reshape(token_count, head_local, key_width)
    grad_value = value_grad_blk.reshape(token_count, head_local, value_width)
    grad_query, grad_key = (
        lax.all_to_all(query_grad_heads, "key", split_axis=2, concat_axis=1, tiled=True),
        lax.all_to_all(key_grad_heads, "key", split_axis=2, concat_axis=1, tiled=True),
    )
    value_square = square_sum(grad_value)
    partial_value = square_sum(grad_query) + square_sum(grad_key) + value_square
    summed = lax.psum(partial_value, ("seq", "key"))
    entries = (
        token_count * lax.axis_size("seq") * query_rows.shape[1] * (2 * key_width + value_width)
    )
    return (grad_query, grad_key, grad_value, summed / entries)


def solution(mesh):
    in_specs = (
        P("seq", None, "key"),
        P("seq", None, "key"),
        P("seq", "key", None),
        P("seq", "key", None),
        P("key", "seq"),
        P("key", "seq"),
        P("seq", "key", None, None),
        P("seq", None, "key", None),
    )
    out_specs = (P("seq", None, "key"), P("seq", None, "key"), P("seq", "key", None), P())
    return jax.shard_map(local, mesh=mesh, in_specs=in_specs, out_specs=out_specs, check_vma=False)
```

profile of v0, /device:TPU:1, one launch (start us, length us, event | category | flops | bytes accessed | tf_op | source)
XLA Modules:
  0.0 631.2 jit_solution(10819537718962490288)
XLA Ops:
  0.7 15.9 %all-to-all-start.1 = ((bf16[256,16,16]{0,2,1:T(8,128)(2,1)}), bf16[256,16,16]{0,2,1:T(8,128)(2,1)S(1)}, u32[]{:S(2)}, u32[]{:S(2)}) async-start(bf16[256,16,16]{0,2,1:T(8,128)(2,1)} %param.15), calls=%async_computation.1 | async-start | bytes 262144 | tf_op jit(solution)/shard_map/all_to_all | solution.py:53
  17.9 10.7 %all-to-all-done.1 = bf16[256,16,16]{0,2,1:T(8,128)(2,1)S(1)} async-done(((bf16[256,16,16]{0,2,1:T(8,128)(2,1)}), bf16[256,16,16]{0,2,1:T(8,128)(2,1)S(1)}, u32[]{:S(2)}, u32[]{:S(2)}) %all-to-all-start.1) | async-done | bytes 131104 | tf_op jit(solution)/shard_map/all_to_all | solution.py:53
  28.6 5.9 all-to-all-start.3
  36.8 9.7 %all-to-all-done.3 = bf16[256,16,16]{0,2,1:T(8,128)(2,1)S(1)} async-done(((bf16[256,16,16]{0,2,1:T(8,128)(2,1)}), bf16[256,16,16]{0,2,1:T(8,128)(2,1)S(1)}, u32[]{:S(2)}, u32[]{:S(2)}) %all-to-all-start.3) | async-done | bytes 131104 | tf_op jit(solution)/shard_map/all_to_all | solution.py:52
  54.0 393.7 %while.57 = (s32[]{:T(128)}, f32[1,256,256]{2,1,0:T(8,128)S(1)}, f32[2,1]{0,1:T(1,128)S(1)}, bf16[2,128,1,256]{3,1,2,0:T(8,128)(2,1)S(1)}, bf16[2,128,1,256]{3,1...) while((s32[]{:T(128)}, f32[1,256,256]{2,1,0:T(8,128)S(1)}, ...), condition=%wide.region_4.5_spmd, body=%wide.region_1.4_spmd.sunk | while | flops 201523200 | bytes 3015986 | solution.py:97
  72.9 5.8 collective-permute-done
  107.3 5.8 collective-permute-done
  118.7 5.8 collective-permute-done
  141.7 5.8 collective-permute-done
  153.1 5.8 collective-permute-done
  210.5 6.5 %collective-permute-done = f32[1,256,256]{2,1,0:T(8,128)S(1)} collective-permute-done((f32[1,256,256]{2,1,0:T(8,128)S(1)}, f32[1,256,256]{2,1,0:T(8,128)S(1)}, u32[]{:S(2)}, u32[]{:S(2)}) %collective-permute-start) | collective-permute-done | bytes 262176 | tf_op jit(solution)/shard_map/while/body/eval_jaxpr/ppermute | solution.py:12
  222.6 7.9 %collective-permute-done = f32[1,256,256]{2,1,0:T(8,128)S(1)} collective-permute-done((f32[1,256,256]{2,1,0:T(8,128)S(1)}, f32[1,256,256]{2,1,0:T(8,128)S(1)}, u32[]{:S(2)}, u32[]{:S(2)}) %collective-permute-start) | collective-permute-done | bytes 262176 | tf_op jit(solution)/shard_map/while/body/eval_jaxpr/ppermute | solution.py:12
  236.2 7.9 %collective-permute-done = f32[1,256,256]{2,1,0:T(8,128)S(1)} collective-permute-done((f32[1,256,256]{2,1,0:T(8,128)S(1)}, f32[1,256,256]{2,1,0:T(8,128)S(1)}, u32[]{:S(2)}, u32[]{:S(2)}) %collective-permute-start) | collective-permute-done | bytes 262176 | tf_op jit(solution)/shard_map/while/body/eval_jaxpr/ppermute | solution.py:12
  249.8 7.9 %collective-permute-done = f32[1,256,256]{2,1,0:T(8,128)S(1)} collective-permute-done((f32[1,256,256]{2,1,0:T(8,128)S(1)}, f32[1,256,256]{2,1,0:T(8,128)S(1)}, u32[]{:S(2)}, u32[]{:S(2)}) %collective-permute-start) | collective-permute-done | bytes 262176 | tf_op jit(solution)/shard_map/while/body/eval_jaxpr/ppermute | solution.py:12
  263.4 7.9 %collective-permute-done = f32[1,256,256]{2,1,0:T(8,128)S(1)} collective-permute-done((f32[1,256,256]{2,1,0:T(8,128)S(1)}, f32[1,256,256]{2,1,0:T(8,128)S(1)}, u32[]{:S(2)}, u32[]{:S(2)}) %collective-permute-start) | collective-permute-done | bytes 262176 | tf_op jit(solution)/shard_map/while/body/eval_jaxpr/ppermute | solution.py:12
  276.9 7.9 %collective-permute-done = f32[1,256,256]{2,1,0:T(8,128)S(1)} collective-permute-done((f32[1,256,256]{2,1,0:T(8,128)S(1)}, f32[1,256,256]{2,1,0:T(8,128)S(1)}, u32[]{:S(2)}, u32[]{:S(2)}) %collective-permute-start) | collective-permute-done | bytes 262176 | tf_op jit(solution)/shard_map/while/body/eval_jaxpr/ppermute | solution.py:12
  290.5 7.9 %collective-permute-done = f32[1,256,256]{2,1,0:T(8,128)S(1)} collective-permute-done((f32[1,256,256]{2,1,0:T(8,128)S(1)}, f32[1,256,256]{2,1,0:T(8,128)S(1)}, u32[]{:S(2)}, u32[]{:S(2)}) %collective-permute-start) | collective-permute-done | bytes 262176 | tf_op jit(solution)/shard_map/while/body/eval_jaxpr/ppermute | solution.py:12
  304.1 7.9 %collective-permute-done = f32[1,256,256]{2,1,0:T(8,128)S(1)} collective-permute-done((f32[1,256,256]{2,1,0:T(8,128)S(1)}, f32[1,256,256]{2,1,0:T(8,128)S(1)}, u32[]{:S(2)}, u32[]{:S(2)}) %collective-permute-start) | collective-permute-done | bytes 262176 | tf_op jit(solution)/shard_map/while/body/eval_jaxpr/ppermute | solution.py:12
  317.7 7.9 %collective-permute-done = f32[1,256,256]{2,1,0:T(8,128)S(1)} collective-permute-done((f32[1,256,256]{2,1,0:T(8,128)S(1)}, f32[1,256,256]{2,1,0:T(8,128)S(1)}, u32[]{:S(2)}, u32[]{:S(2)}) %collective-permute-start) | collective-permute-done | bytes 262176 | tf_op jit(solution)/shard_map/while/body/eval_jaxpr/ppermute | solution.py:12
  331.2 7.9 %collective-permute-done = f32[1,256,256]{2,1,0:T(8,128)S(1)} collective-permute-done((f32[1,256,256]{2,1,0:T(8,128)S(1)}, f32[1,256,256]{2,1,0:T(8,128)S(1)}, u32[]{:S(2)}, u32[]{:S(2)}) %collective-permute-start) | collective-permute-done | bytes 262176 | tf_op jit(solution)/shard_map/while/body/eval_jaxpr/ppermute | solution.py:12
  344.8 7.9 %collective-permute-done = f32[1,256,256]{2,1,0:T(8,128)S(1)} collective-permute-done((f32[1,256,256]{2,1,0:T(8,128)S(1)}, f32[1,256,256]{2,1,0:T(8,128)S(1)}, u32[]{:S(2)}, u32[]{:S(2)}) %collective-permute-start) | collective-permute-done | bytes 262176 | tf_op jit(solution)/shard_map/while/body/eval_jaxpr/ppermute | solution.py:12
  358.4 7.9 %collective-permute-done = f32[1,256,256]{2,1,0:T(8,128)S(1)} collective-permute-done((f32[1,256,256]{2,1,0:T(8,128)S(1)}, f32[1,256,256]{2,1,0:T(8,128)S(1)}, u32[]{:S(2)}, u32[]{:S(2)}) %collective-permute-start) | collective-permute-done | bytes 262176 | tf_op jit(solution)/shard_map/while/body/eval_jaxpr/ppermute | solution.py:12
  372.0 7.9 %collective-permute-done = f32[1,256,256]{2,1,0:T(8,128)S(1)} collective-permute-done((f32[1,256,256]{2,1,0:T(8,128)S(1)}, f32[1,256,256]{2,1,0:T(8,128)S(1)}, u32[]{:S(2)}, u32[]{:S(2)}) %collective-permute-start) | collective-permute-done | bytes 262176 | tf_op jit(solution)/shard_map/while/body/eval_jaxpr/ppermute | solution.py:12
  385.5 7.9 %collective-permute-done = f32[1,256,256]{2,1,0:T(8,128)S(1)} collective-permute-done((f32[1,256,256]{2,1,0:T(8,128)S(1)}, f32[1,256,256]{2,1,0:T(8,128)S(1)}, u32[]{:S(2)}, u32[]{:S(2)}) %collective-permute-start) | collective-permute-done | bytes 262176 | tf_op jit(solution)/shard_map/while/body/eval_jaxpr/ppermute | solution.py:12
  399.1 7.9 %collective-permute-done = f32[1,256,256]{2,1,0:T(8,128)S(1)} collective-permute-done((f32[1,256,256]{2,1,0:T(8,128)S(1)}, f32[1,256,256]{2,1,0:T(8,128)S(1)}, u32[]{:S(2)}, u32[]{:S(2)}) %collective-permute-start) | collective-permute-done | bytes 262176 | tf_op jit(solution)/shard_map/while/body/eval_jaxpr/ppermute | solution.py:12
  412.7 7.9 %collective-permute-done = f32[1,256,256]{2,1,0:T(8,128)S(1)} collective-permute-done((f32[1,256,256]{2,1,0:T(8,128)S(1)}, f32[1,256,256]{2,1,0:T(8,128)S(1)}, u32[]{:S(2)}, u32[]{:S(2)}) %collective-permute-start) | collective-permute-done | bytes 262176 | tf_op jit(solution)/shard_map/while/body/eval_jaxpr/ppermute | solution.py:12
  426.2 7.9 %collective-permute-done = f32[1,256,256]{2,1,0:T(8,128)S(1)} collective-permute-done((f32[1,256,256]{2,1,0:T(8,128)S(1)}, f32[1,256,256]{2,1,0:T(8,128)S(1)}, u32[]{:S(2)}, u32[]{:S(2)}) %collective-permute-start) | collective-permute-done | bytes 262176 | tf_op jit(solution)/shard_map/while/body/eval_jaxpr/ppermute | solution.py:12
  439.8 7.9 %collective-permute-done = f32[1,256,256]{2,1,0:T(8,128)S(1)} collective-permute-done((f32[1,256,256]{2,1,0:T(8,128)S(1)}, f32[1,256,256]{2,1,0:T(8,128)S(1)}, u32[]{:S(2)}, u32[]{:S(2)}) %collective-permute-start) | collective-permute-done | bytes 262176 | tf_op jit(solution)/shard_map/while/body/eval_jaxpr/ppermute | solution.py:12
  456.1 11.2 %all-to-all-start.4 = ((bf16[16,2,2048]{2,1,0:T(2,128)(2,1)}), bf16[16,2,2048]{2,1,0:T(2,128)(2,1)S(1)}, u32[]{:S(2)}, u32[]{:S(2)}) async-start(bf16[16,2,2048]{2,1,0:T(2,128)(2,1)} %reshape.369), calls=%async_computation.4 | async-start | bytes 262144 | tf_op jit(solution)/shard_map/all_to_all | solution.py:127
  470.0 9.2 %all-to-all-done.4 = bf16[16,2,2048]{2,1,0:T(2,128)(2,1)S(1)} async-done(((bf16[16,2,2048]{2,1,0:T(2,128)(2,1)}), bf16[16,2,2048]{2,1,0:T(2,128)(2,1)S(1)}, u32[]{:S(2)}, u32[]{:S(2)}) %all-to-all-start.4) | async-done | bytes 131104 | tf_op jit(solution)/shard_map/all_to_all | solution.py:127
  484.6 10.4 %all-to-all-done.2 = bf16[16,2,2048]{2,1,0:T(2,128)(2,1)S(1)} async-done(((bf16[16,2,2048]{2,1,0:T(2,128)(2,1)}), bf16[16,2,2048]{2,1,0:T(2,128)(2,1)S(1)}, u32[]{:S(2)}, u32[]{:S(2)}) %all-to-all-start.2) | async-done | bytes 131104 | tf_op jit(solution)/shard_map/all_to_all | solution.py:126
  498.3 129.8 %psum.7 = f32[]{:T(128)} all-reduce(f32[]{:T(128)S(6)} %add.89), channel_id=1, replica_groups=mesh['seq'=32,'key'=16] {'seq','key'}, use_global_device_ids=true, to_apply=%region_10.11 | all-reduce | flops 1 | bytes 8 | tf_op jit(solution)/shard_map/psum | solution.py:131
  (355 shorter events, 371.1 us)
Async XLA Ops:
  0.7 27.9 %all-to-all-start.1 = ((bf16[256,16,16]{0,2,1:T(8,128)(2,1)}), bf16[256,16,16]{0,2,1:T(8,128)(2,1)S(1)}, u32[]{:S(2)}, u32[]{:S(2)}) async-start(bf16[256,16,16]{0,2,1:T(8,128)(2,1)} %param.15), calls=%async_computation.1 | async-start | bytes 262144 | tf_op jit(solution)/shard_map/all_to_all | solution.py:53
  28.6 17.9 %all-to-all-start.3 = ((bf16[256,16,16]{0,2,1:T(8,128)(2,1)}), bf16[256,16,16]{0,2,1:T(8,128)(2,1)S(1)}, u32[]{:S(2)}, u32[]{:S(2)}) async-start(bf16[256,16,16]{0,2,1:T(8,128)(2,1)} %param.14), calls=%async_computation.3 | async-start | bytes 262144 | tf_op jit(solution)/shard_map/all_to_all | solution.py:52
  46.5 405.4 %all-to-all-start = ((bf16[2,16,16,256]{3,2,0,1:T(8,128)(2,1)}), bf16[2,16,16,256]{3,2,0,1:T(8,128)(2,1)S(1)}, u32[]{:S(2)}, u32[]{:S(2)}) async-start(bf16[2,16,16,256]{3,2,0,1:T(8,128)(2,1)} %copy.117), calls=%async_computation | async-start | bytes 524288 | tf_op jit(solution)/shard_map/all_to_all | solution.py:54
  57.7 9.4 %collective-permute-start = (f32[1,256,256]{2,1,0:T(8,128)S(1)}, f32[1,256,256]{2,1,0:T(8,128)S(1)}, u32[]{:S(2)}, u32[]{:S(2)}) collective-permute-start(f32[1,256,256]{2,1,0:T(8,128)S(1)} %get-tuple-element.637), channel_id=1, source_target_pairs={{16,0},{32,16},{48,32},{64,48},{80,64},{96,80},{112,96},{128,112},... | collective-permute-start | bytes 786440 | tf_op jit(solution)/shard_map/while/body/eval_jaxpr/ppermute | solution.py:12
  71.0 7.7 %collective-permute-start = (f32[1,256,256]{2,1,0:T(8,128)S(1)}, f32[1,256,256]{2,1,0:T(8,128)S(1)}, u32[]{:S(2)}, u32[]{:S(2)}) collective-permute-start(f32[1,256,256]{2,1,0:T(8,128)S(1)} %get-tuple-element.637), channel_id=1, source_target_pairs={{16,0},{32,16},{48,32},{64,48},{80,64},{96,80},{112,96},{128,112},... | collective-permute-start | bytes 786440 | tf_op jit(solution)/shard_map/while/body/eval_jaxpr/ppermute | solution.py:12
  82.4 7.7 %collective-permute-start = (f32[1,256,256]{2,1,0:T(8,128)S(1)}, f32[1,256,256]{2,1,0:T(8,128)S(1)}, u32[]{:S(2)}, u32[]{:S(2)}) collective-permute-start(f32[1,256,256]{2,1,0:T(8,128)S(1)} %get-tuple-element.637), channel_id=1, source_target_pairs={{16,0},{32,16},{48,32},{64,48},{80,64},{96,80},{112,96},{128,112},... | collective-permute-start | bytes 786440 | tf_op jit(solution)/shard_map/while/body/eval_jaxpr/ppermute | solution.py:12
  105.4 7.7 %collective-permute-start = (f32[1,256,256]{2,1,0:T(8,128)S(1)}, f32[1,256,256]{2,1,0:T(8,128)S(1)}, u32[]{:S(2)}, u32[]{:S(2)}) collective-permute-start(f32[1,256,256]{2,1,0:T(8,128)S(1)} %get-tuple-element.637), channel_id=1, source_target_pairs={{16,0},{32,16},{48,32},{64,48},{80,64},{96,80},{112,96},{128,112},... | collective-permute-start | bytes 786440 | tf_op jit(solution)/shard_map/while/body/eval_jaxpr/ppermute | solution.py:12
  116.8 7.7 %collective-permute-start = (f32[1,256,256]{2,1,0:T(8,128)S(1)}, f32[1,256,256]{2,1,0:T(8,128)S(1)}, u32[]{:S(2)}, u32[]{:S(2)}) collective-permute-start(f32[1,256,256]{2,1,0:T(8,128)S(1)} %get-tuple-element.637), channel_id=1, source_target_pairs={{16,0},{32,16},{48,32},{64,48},{80,64},{96,80},{112,96},{128,112},... | collective-permute-start | bytes 786440 | tf_op jit(solution)/shard_map/while/body/eval_jaxpr/ppermute | solution.py:12
  139.7 7.7 %collective-permute-start = (f32[1,256,256]{2,1,0:T(8,128)S(1)}, f32[1,256,256]{2,1,0:T(8,128)S(1)}, u32[]{:S(2)}, u32[]{:S(2)}) collective-permute-start(f32[1,256,256]{2,1,0:T(8,128)S(1)} %get-tuple-element.637), channel_id=1, source_target_pairs={{16,0},{32,16},{48,32},{64,48},{80,64},{96,80},{112,96},{128,112},... | collective-permute-start | bytes 786440 | tf_op jit(solution)/shard_map/while/body/eval_jaxpr/ppermute | solution.py:12
  151.2 7.7 %collective-permute-start = (f32[1,256,256]{2,1,0:T(8,128)S(1)}, f32[1,256,256]{2,1,0:T(8,128)S(1)}, u32[]{:S(2)}, u32[]{:S(2)}) collective-permute-start(f32[1,256,256]{2,1,0:T(8,128)S(1)} %get-tuple-element.637), channel_id=1, source_target_pairs={{16,0},{32,16},{48,32},{64,48},{80,64},{96,80},{112,96},{128,112},... | collective-permute-start | bytes 786440 | tf_op jit(solution)/shard_map/while/body/eval_jaxpr/ppermute | solution.py:12
  174.1 7.7 %collective-permute-start = (f32[1,256,256]{2,1,0:T(8,128)S(1)}, f32[1,256,256]{2,1,0:T(8,128)S(1)}, u32[]{:S(2)}, u32[]{:S(2)}) collective-permute-start(f32[1,256,256]{2,1,0:T(8,128)S(1)} %get-tuple-element.637), channel_id=1, source_target_pairs={{16,0},{32,16},{48,32},{64,48},{80,64},{96,80},{112,96},{128,112},... | collective-permute-start | bytes 786440 | tf_op jit(solution)/shard_map/while/body/eval_jaxpr/ppermute | solution.py:12
  185.6 7.7 %collective-permute-start = (f32[1,256,256]{2,1,0:T(8,128)S(1)}, f32[1,256,256]{2,1,0:T(8,128)S(1)}, u32[]{:S(2)}, u32[]{:S(2)}) collective-permute-start(f32[1,256,256]{2,1,0:T(8,128)S(1)} %get-tuple-element.637), channel_id=1, source_target_pairs={{16,0},{32,16},{48,32},{64,48},{80,64},{96,80},{112,96},{128,112},... | collective-permute-start | bytes 786440 | tf_op jit(solution)/shard_map/while/body/eval_jaxpr/ppermute | solution.py:12
  208.5 8.4 %collective-permute-start = (f32[1,256,256]{2,1,0:T(8,128)S(1)}, f32[1,256,256]{2,1,0:T(8,128)S(1)}, u32[]{:S(2)}, u32[]{:S(2)}) collective-permute-start(f32[1,256,256]{2,1,0:T(8,128)S(1)} %get-tuple-element.637), channel_id=1, source_target_pairs={{16,0},{32,16},{48,32},{64,48},{80,64},{96,80},{112,96},{128,112},... | collective-permute-start | bytes 786440 | tf_op jit(solution)/shard_map/while/body/eval_jaxpr/ppermute | solution.py:12
  220.7 9.8 %collective-permute-start = (f32[1,256,256]{2,1,0:T(8,128)S(1)}, f32[1,256,256]{2,1,0:T(8,128)S(1)}, u32[]{:S(2)}, u32[]{:S(2)}) collective-permute-start(f32[1,256,256]{2,1,0:T(8,128)S(1)} %get-tuple-element.637), channel_id=1, source_target_pairs={{16,0},{32,16},{48,32},{64,48},{80,64},{96,80},{112,96},{128,112},... | collective-permute-start | bytes 786440 | tf_op jit(solution)/shard_map/while/body/eval_jaxpr/ppermute | solution.py:12
  234.3 9.8 %collective-permute-start = (f32[1,256,256]{2,1,0:T(8,128)S(1)}, f32[1,256,256]{2,1,0:T(8,128)S(1)}, u32[]{:S(2)}, u32[]{:S(2)}) collective-permute-start(f32[1,256,256]{2,1,0:T(8,128)S(1)} %get-tuple-element.637), channel_id=1, source_target_pairs={{16,0},{32,16},{48,32},{64,48},{80,64},{96,80},{112,96},{128,112},... | collective-permute-start | bytes 786440 | tf_op jit(solution)/shard_map/while/body/eval_jaxpr/ppermute | solution.py:12
  247.9 9.8 %collective-permute-start = (f32[1,256,256]{2,1,0:T(8,128)S(1)}, f32[1,256,256]{2,1,0:T(8,128)S(1)}, u32[]{:S(2)}, u32[]{:S(2)}) collective-permute-start(f32[1,256,256]{2,1,0:T(8,128)S(1)} %get-tuple-element.637), channel_id=1, source_target_pairs={{16,0},{32,16},{48,32},{64,48},{80,64},{96,80},{112,96},{128,112},... | collective-permute-start | bytes 786440 | tf_op jit(solution)/shard_map/while/body/eval_jaxpr/ppermute | solution.py:12
  261.4 9.8 %collective-permute-start = (f32[1,256,256]{2,1,0:T(8,128)S(1)}, f32[1,256,256]{2,1,0:T(8,128)S(1)}, u32[]{:S(2)}, u32[]{:S(2)}) collective-permute-start(f32[1,256,256]{2,1,0:T(8,128)S(1)} %get-tuple-element.637), channel_id=1, source_target_pairs={{16,0},{32,16},{48,32},{64,48},{80,64},{96,80},{112,96},{128,112},... | collective-permute-start | bytes 786440 | tf_op jit(solution)/shard_map/while/body/eval_jaxpr/ppermute | solution.py:12
  275.0 9.8 %collective-permute-start = (f32[1,256,256]{2,1,0:T(8,128)S(1)}, f32[1,256,256]{2,1,0:T(8,128)S(1)}, u32[]{:S(2)}, u32[]{:S(2)}) collective-permute-start(f32[1,256,256]{2,1,0:T(8,128)S(1)} %get-tuple-element.637), channel_id=1, source_target_pairs={{16,0},{32,16},{48,32},{64,48},{80,64},{96,80},{112,96},{128,112},... | collective-permute-start | bytes 786440 | tf_op jit(solution)/shard_map/while/body/eval_jaxpr/ppermute | solution.py:12
  288.6 9.8 %collective-permute-start = (f32[1,256,256]{2,1,0:T(8,128)S(1)}, f32[1,256,256]{2,1,0:T(8,128)S(1)}, u32[]{:S(2)}, u32[]{:S(2)}) collective-permute-start(f32[1,256,256]{2,1,0:T(8,128)S(1)} %get-tuple-element.637), channel_id=1, source_target_pairs={{16,0},{32,16},{48,32},{64,48},{80,64},{96,80},{112,96},{128,112},... | collective-permute-start | bytes 786440 | tf_op jit(solution)/shard_map/while/body/eval_jaxpr/ppermute | solution.py:12
  302.2 9.8 %collective-permute-start = (f32[1,256,256]{2,1,0:T(8,128)S(1)}, f32[1,256,256]{2,1,0:T(8,128)S(1)}, u32[]{:S(2)}, u32[]{:S(2)}) collective-permute-start(f32[1,256,256]{2,1,0:T(8,128)S(1)} %get-tuple-element.637), channel_id=1, source_target_pairs={{16,0},{32,16},{48,32},{64,48},{80,64},{96,80},{112,96},{128,112},... | collective-permute-start | bytes 786440 | tf_op jit(solution)/shard_map/while/body/eval_jaxpr/ppermute | solution.py:12
  315.7 9.8 %collective-permute-start = (f32[1,256,256]{2,1,0:T(8,128)S(1)}, f32[1,256,256]{2,1,0:T(8,128)S(1)}, u32[]{:S(2)}, u32[]{:S(2)}) collective-permute-start(f32[1,256,256]{2,1,0:T(8,128)S(1)} %get-tuple-element.637), channel_id=1, source_target_pairs={{16,0},{32,16},{48,32},{64,48},{80,64},{96,80},{112,96},{128,112},... | collective-permute-start | bytes 786440 | tf_op jit(solution)/shard_map/while/body/eval_jaxpr/ppermute | solution.py:12
  329.3 9.8 %collective-permute-start = (f32[1,256,256]{2,1,0:T(8,128)S(1)}, f32[1,256,256]{2,1,0:T(8,128)S(1)}, u32[]{:S(2)}, u32[]{:S(2)}) collective-permute-start(f32[1,256,256]{2,1,0:T(8,128)S(1)} %get-tuple-element.637), channel_id=1, source_target_pairs={{16,0},{32,16},{48,32},{64,48},{80,64},{96,80},{112,96},{128,112},... | collective-permute-start | bytes 786440 | tf_op jit(solution)/shard_map/while/body/eval_jaxpr/ppermute | solution.py:12
  342.9 9.8 %collective-permute-start = (f32[1,256,256]{2,1,0:T(8,128)S(1)}, f32[1,256,256]{2,1,0:T(8,128)S(1)}, u32[]{:S(2)}, u32[]{:S(2)}) collective-permute-start(f32[1,256,256]{2,1,0:T(8,128)S(1)} %get-tuple-element.637), channel_id=1, source_target_pairs={{16,0},{32,16},{48,32},{64,48},{80,64},{96,80},{112,96},{128,112},... | collective-permute-start | bytes 786440 | tf_op jit(solution)/shard_map/while/body/eval_jaxpr/ppermute | solution.py:12
  356.5 9.8 %collective-permute-start = (f32[1,256,256]{2,1,0:T(8,128)S(1)}, f32[1,256,256]{2,1,0:T(8,128)S(1)}, u32[]{:S(2)}, u32[]{:S(2)}) collective-permute-start(f32[1,256,256]{2,1,0:T(8,128)S(1)} %get-tuple-element.637), channel_id=1, source_target_pairs={{16,0},{32,16},{48,32},{64,48},{80,64},{96,80},{112,96},{128,112},... | collective-permute-start | bytes 786440 | tf_op jit(solution)/shard_map/while/body/eval_jaxpr/ppermute | solution.py:12
  370.0 9.8 %collective-permute-start = (f32[1,256,256]{2,1,0:T(8,128)S(1)}, f32[1,256,256]{2,1,0:T(8,128)S(1)}, u32[]{:S(2)}, u32[]{:S(2)}) collective-permute-start(f32[1,256,256]{2,1,0:T(8,128)S(1)} %get-tuple-element.637), channel_id=1, source_target_pairs={{16,0},{32,16},{48,32},{64,48},{80,64},{96,80},{112,96},{128,112},... | collective-permute-start | bytes 786440 | tf_op jit(solution)/shard_map/while/body/eval_jaxpr/ppermute | solution.py:12
  383.6 9.8 %collective-permute-start = (f32[1,256,256]{2,1,0:T(8,128)S(1)}, f32[1,256,256]{2,1,0:T(8,128)S(1)}, u32[]{:S(2)}, u32[]{:S(2)}) collective-permute-start(f32[1,256,256]{2,1,0:T(8,128)S(1)} %get-tuple-element.637), channel_id=1, source_target_pairs={{16,0},{32,16},{48,32},{64,48},{80,64},{96,80},{112,96},{128,112},... | collective-permute-start | bytes 786440 | tf_op jit(solution)/shard_map/while/body/eval_jaxpr/ppermute | solution.py:12
  397.2 9.8 %collective-permute-start = (f32[1,256,256]{2,1,0:T(8,128)S(1)}, f32[1,256,256]{2,1,0:T(8,128)S(1)}, u32[]{:S(2)}, u32[]{:S(2)}) collective-permute-start(f32[1,256,256]{2,1,0:T(8,128)S(1)} %get-tuple-element.637), channel_id=1, source_target_pairs={{16,0},{32,16},{48,32},{64,48},{80,64},{96,80},{112,96},{128,112},... | collective-permute-start | bytes 786440 | tf_op jit(solution)/shard_map/while/body/eval_jaxpr/ppermute | solution.py:12
  410.7 9.8 %collective-permute-start = (f32[1,256,256]{2,1,0:T(8,128)S(1)}, f32[1,256,256]{2,1,0:T(8,128)S(1)}, u32[]{:S(2)}, u32[]{:S(2)}) collective-permute-start(f32[1,256,256]{2,1,0:T(8,128)S(1)} %get-tuple-element.637), channel_id=1, source_target_pairs={{16,0},{32,16},{48,32},{64,48},{80,64},{96,80},{112,96},{128,112},... | collective-permute-start | bytes 786440 | tf_op jit(solution)/shard_map/while/body/eval_jaxpr/ppermute | solution.py:12
  424.3 9.8 %collective-permute-start = (f32[1,256,256]{2,1,0:T(8,128)S(1)}, f32[1,256,256]{2,1,0:T(8,128)S(1)}, u32[]{:S(2)}, u32[]{:S(2)}) collective-permute-start(f32[1,256,256]{2,1,0:T(8,128)S(1)} %get-tuple-element.637), channel_id=1, source_target_pairs={{16,0},{32,16},{48,32},{64,48},{80,64},{96,80},{112,96},{128,112},... | collective-permute-start | bytes 786440 | tf_op jit(solution)/shard_map/while/body/eval_jaxpr/ppermute | solution.py:12
  437.9 9.8 %collective-permute-start = (f32[1,256,256]{2,1,0:T(8,128)S(1)}, f32[1,256,256]{2,1,0:T(8,128)S(1)}, u32[]{:S(2)}, u32[]{:S(2)}) collective-permute-start(f32[1,256,256]{2,1,0:T(8,128)S(1)} %get-tuple-element.637), channel_id=1, source_target_pairs={{16,0},{32,16},{48,32},{64,48},{80,64},{96,80},{112,96},{128,112},... | collective-permute-start | bytes 786440 | tf_op jit(solution)/shard_map/while/body/eval_jaxpr/ppermute | solution.py:12
  456.1 23.1 %all-to-all-start.4 = ((bf16[16,2,2048]{2,1,0:T(2,128)(2,1)}), bf16[16,2,2048]{2,1,0:T(2,128)(2,1)S(1)}, u32[]{:S(2)}, u32[]{:S(2)}) async-start(bf16[16,2,2048]{2,1,0:T(2,128)(2,1)} %reshape.369), calls=%async_computation.4 | async-start | bytes 262144 | tf_op jit(solution)/shard_map/all_to_all | solution.py:127
  479.2 15.8 %all-to-all-start.2 = ((bf16[16,2,2048]{2,1,0:T(2,128)(2,1)}), bf16[16,2,2048]{2,1,0:T(2,128)(2,1)S(1)}, u32[]{:S(2)}, u32[]{:S(2)}) async-start(bf16[16,2,2048]{2,1,0:T(2,128)(2,1)} %reshape.367), calls=%async_computation.2 | async-start | bytes 262144 | tf_op jit(solution)/shard_map/all_to_all | solution.py:126
  (10 other events, 119.9 us)
where the time goes:
time: 636 us; the launch traced here: 631 us
  waiting for transfers between devices  255 us (40%)
  blocking collectives  130 us (20%)
  starting transfers between devices  104 us (16%)
  matrix products  84.9 us (13%)
  local copies, waits for them, and re-layouts  45.3 us (7%)
    ppermute x31, waiting for transfers between devices, from_behind(): lax.ppermute(value, axis, [(source, source + steps) for source in range(f...  215 us
    psum x1, blocking collectives, local(): summed = lax.psum(partial_value, ('seq', 'key'))  130 us
    dot_general x130, matrix products, precise_product(): jnp.einsum(form, left.astype(jnp.float32), right, precision=highest_mode)  80.6 us
    ppermute x31, starting transfers between devices, from_behind(): lax.ppermute(value, axis, [(source, source + steps) for source in range(f...  61.5 us
    dynamic_slice x64, local copies, waits for them, and re-layouts, device_map(): lax.scan(group_step, state_out, (written_keys, key_result, end_decay, off...  37.6 us
    all_to_all x1, starting transfers between devices, local(): lax.all_to_all(key_rows, 'key', split_axis=1, concat_axis=2, tiled=True)  15.9 us
  transfers between devices with their start and end apart: 36, of which 35 were waited for; matrix products, arithmetic and copies ran while one was open for 20% of the time, Pallas kernels for 0%

commit v1 on v0

--- a/solution.py
+++ b/solution.py
@@ -128,7 +128,8 @@
     )
     value_square = square_sum(grad_value)
     partial_value = square_sum(grad_query) + square_sum(grad_key) + value_square
-    summed = lax.psum(partial_value, ("seq", "key"))
+    extra = jax.lax.psum(partial_value, "key")
+    summed = jax.lax.psum(extra, "seq")
     entries = (
         token_count * lax.axis_size("seq") * query_rows.shape[1] * (2 * key_width + value_width)
     )

time: 636 us -> 618 us (0.972)
  blocking collectives: 130 us -> 107 us
    psum x1 -> x2, blocking collectives: 130 us -> 107 us  [the longest x1 85.1 us: local(): summed = jax.lax.psum(extra, 'seq')]
  transfers between devices with their start and end apart: 36 -> 36, of which waited for: 35 -> 35; matrix products, arithmetic and copies ran while one was open for 20% -> 21% of each run, Pallas kernels for 0% -> 0%
where the time goes in v1:
time: 618 us; the launch traced here: 609 us
  waiting for transfers between devices  255 us (41%)
  blocking collectives  107 us (17%)
  starting transfers between devices  104 us (17%)
  matrix products  84.9 us (14%)
  local copies, waits for them, and re-layouts  45.3 us (7%)
    ppermute x31, waiting for transfers between devices, from_behind(): lax.ppermute(value, axis, [(source, source + steps) for source in range(f...  215 us
    psum x1, blocking collectives, local(): summed = jax.lax.psum(extra, 'seq')  85.1 us
    dot_general x130, matrix products, precise_product(): jnp.einsum(form, left.astype(jnp.float32), right, precision=highest_mode)  80.6 us
    ppermute x31, starting transfers between devices, from_behind(): lax.ppermute(value, axis, [(source, source + steps) for source in range(f...  61.5 us
    dynamic_slice x64, local copies, waits for them, and re-layouts, device_map(): lax.scan(group_step, state_out, (written_keys, key_result, end_decay, off...  37.6 us
    psum x1, blocking collectives, local(): extra = jax.lax.psum(partial_value, 'key')  22.3 us
    all_to_all x1, starting transfers between devices, local(): lax.all_to_all(key_rows, 'key', split_axis=1, concat_axis=2, tiled=True)  15.9 us
  transfers between devices with their start and end apart: 36, of which 35 were waited for; matrix products, arithmetic and copies ran while one was open for 21% of the time, Pallas kernels for 0%

profile of v1, /device:TPU:1, one launch (start us, length us, event | category | flops | bytes accessed | tf_op | source)
XLA Modules:
  0.0 608.8 jit_solution(8813328961810145554)
XLA Ops:
  0.7 15.9 %all-to-all-start.1 = ((bf16[256,16,16]{0,2,1:T(8,128)(2,1)}), bf16[256,16,16]{0,2,1:T(8,128)(2,1)S(1)}, u32[]{:S(2)}, u32[]{:S(2)}) async-start(bf16[256,16,16]{0,2,1:T(8,128)(2,1)} %param.15), calls=%async_computation.1 | async-start | bytes 262144 | tf_op jit(solution)/shard_map/all_to_all | solution.py:53
  17.9 10.7 %all-to-all-done.1 = bf16[256,16,16]{0,2,1:T(8,128)(2,1)S(1)} async-done(((bf16[256,16,16]{0,2,1:T(8,128)(2,1)}), bf16[256,16,16]{0,2,1:T(8,128)(2,1)S(1)}, u32[]{:S(2)}, u32[]{:S(2)}) %all-to-all-start.1) | async-done | bytes 131104 | tf_op jit(solution)/shard_map/all_to_all | solution.py:53
  28.6 5.9 all-to-all-start.3
  36.8 9.7 %all-to-all-done.3 = bf16[256,16,16]{0,2,1:T(8,128)(2,1)S(1)} async-done(((bf16[256,16,16]{0,2,1:T(8,128)(2,1)}), bf16[256,16,16]{0,2,1:T(8,128)(2,1)S(1)}, u32[]{:S(2)}, u32[]{:S(2)}) %all-to-all-start.3) | async-done | bytes 131104 | tf_op jit(solution)/shard_map/all_to_all | solution.py:52
  54.0 393.7 %while.57 = (s32[]{:T(128)}, f32[1,256,256]{2,1,0:T(8,128)S(1)}, f32[2,1]{0,1:T(1,128)S(1)}, bf16[2,128,1,256]{3,1,2,0:T(8,128)(2,1)S(1)}, bf16[2,128,1,256]{3,1...) while((s32[]{:T(128)}, f32[1,256,256]{2,1,0:T(8,128)S(1)}, ...), condition=%wide.region_4.5_spmd, body=%wide.region_1.4_spmd.sunk | while | flops 201523200 | bytes 3015986 | solution.py:97
  72.9 5.8 collective-permute-done
  107.3 5.8 collective-permute-done
  118.7 5.8 collective-permute-done
  141.7 5.8 collective-permute-done
  210.5 6.5 %collective-permute-done = f32[1,256,256]{2,1,0:T(8,128)S(1)} collective-permute-done((f32[1,256,256]{2,1,0:T(8,128)S(1)}, f32[1,256,256]{2,1,0:T(8,128)S(1)}, u32[]{:S(2)}, u32[]{:S(2)}) %collective-permute-start) | collective-permute-done | bytes 262176 | tf_op jit(solution)/shard_map/while/body/eval_jaxpr/ppermute | solution.py:12
  222.6 7.9 %collective-permute-done = f32[1,256,256]{2,1,0:T(8,128)S(1)} collective-permute-done((f32[1,256,256]{2,1,0:T(8,128)S(1)}, f32[1,256,256]{2,1,0:T(8,128)S(1)}, u32[]{:S(2)}, u32[]{:S(2)}) %collective-permute-start) | collective-permute-done | bytes 262176 | tf_op jit(solution)/shard_map/while/body/eval_jaxpr/ppermute | solution.py:12
  236.2 7.9 %collective-permute-done = f32[1,256,256]{2,1,0:T(8,128)S(1)} collective-permute-done((f32[1,256,256]{2,1,0:T(8,128)S(1)}, f32[1,256,256]{2,1,0:T(8,128)S(1)}, u32[]{:S(2)}, u32[]{:S(2)}) %collective-permute-start) | collective-permute-done | bytes 262176 | tf_op jit(solution)/shard_map/while/body/eval_jaxpr/ppermute | solution.py:12
  249.8 7.9 %collective-permute-done = f32[1,256,256]{2,1,0:T(8,128)S(1)} collective-permute-done((f32[1,256,256]{2,1,0:T(8,128)S(1)}, f32[1,256,256]{2,1,0:T(8,128)S(1)}, u32[]{:S(2)}, u32[]{:S(2)}) %collective-permute-start) | collective-permute-done | bytes 262176 | tf_op jit(solution)/shard_map/while/body/eval_jaxpr/ppermute | solution.py:12
  263.4 7.9 %collective-permute-done = f32[1,256,256]{2,1,0:T(8,128)S(1)} collective-permute-done((f32[1,256,256]{2,1,0:T(8,128)S(1)}, f32[1,256,256]{2,1,0:T(8,128)S(1)}, u32[]{:S(2)}, u32[]{:S(2)}) %collective-permute-start) | collective-permute-done | bytes 262176 | tf_op jit(solution)/shard_map/while/body/eval_jaxpr/ppermute | solution.py:12
  276.9 7.9 %collective-permute-done = f32[1,256,256]{2,1,0:T(8,128)S(1)} collective-permute-done((f32[1,256,256]{2,1,0:T(8,128)S(1)}, f32[1,256,256]{2,1,0:T(8,128)S(1)}, u32[]{:S(2)}, u32[]{:S(2)}) %collective-permute-start) | collective-permute-done | bytes 262176 | tf_op jit(solution)/shard_map/while/body/eval_jaxpr/ppermute | solution.py:12
  290.5 7.9 %collective-permute-done = f32[1,256,256]{2,1,0:T(8,128)S(1)} collective-permute-done((f32[1,256,256]{2,1,0:T(8,128)S(1)}, f32[1,256,256]{2,1,0:T(8,128)S(1)}, u32[]{:S(2)}, u32[]{:S(2)}) %collective-permute-start) | collective-permute-done | bytes 262176 | tf_op jit(solution)/shard_map/while/body/eval_jaxpr/ppermute | solution.py:12
  304.1 7.9 %collective-permute-done = f32[1,256,256]{2,1,0:T(8,128)S(1)} collective-permute-done((f32[1,256,256]{2,1,0:T(8,128)S(1)}, f32[1,256,256]{2,1,0:T(8,128)S(1)}, u32[]{:S(2)}, u32[]{:S(2)}) %collective-permute-start) | collective-permute-done | bytes 262176 | tf_op jit(solution)/shard_map/while/body/eval_jaxpr/ppermute | solution.py:12
  317.7 7.9 %collective-permute-done = f32[1,256,256]{2,1,0:T(8,128)S(1)} collective-permute-done((f32[1,256,256]{2,1,0:T(8,128)S(1)}, f32[1,256,256]{2,1,0:T(8,128)S(1)}, u32[]{:S(2)}, u32[]{:S(2)}) %collective-permute-start) | collective-permute-done | bytes 262176 | tf_op jit(solution)/shard_map/while/body/eval_jaxpr/ppermute | solution.py:12
  331.2 7.9 %collective-permute-done = f32[1,256,256]{2,1,0:T(8,128)S(1)} collective-permute-done((f32[1,256,256]{2,1,0:T(8,128)S(1)}, f32[1,256,256]{2,1,0:T(8,128)S(1)}, u32[]{:S(2)}, u32[]{:S(2)}) %collective-permute-start) | collective-permute-done | bytes 262176 | tf_op jit(solution)/shard_map/while/body/eval_jaxpr/ppermute | solution.py:12
  344.8 7.9 %collective-permute-done = f32[1,256,256]{2,1,0:T(8,128)S(1)} collective-permute-done((f32[1,256,256]{2,1,0:T(8,128)S(1)}, f32[1,256,256]{2,1,0:T(8,128)S(1)}, u32[]{:S(2)}, u32[]{:S(2)}) %collective-permute-start) | collective-permute-done | bytes 262176 | tf_op jit(solution)/shard_map/while/body/eval_jaxpr/ppermute | solution.py:12
  358.4 7.9 %collective-permute-done = f32[1,256,256]{2,1,0:T(8,128)S(1)} collective-permute-done((f32[1,256,256]{2,1,0:T(8,128)S(1)}, f32[1,256,256]{2,1,0:T(8,128)S(1)}, u32[]{:S(2)}, u32[]{:S(2)}) %collective-permute-start) | collective-permute-done | bytes 262176 | tf_op jit(solution)/shard_map/while/body/eval_jaxpr/ppermute | solution.py:12
  372.0 7.9 %collective-permute-done = f32[1,256,256]{2,1,0:T(8,128)S(1)} collective-permute-done((f32[1,256,256]{2,1,0:T(8,128)S(1)}, f32[1,256,256]{2,1,0:T(8,128)S(1)}, u32[]{:S(2)}, u32[]{:S(2)}) %collective-permute-start) | collective-permute-done | bytes 262176 | tf_op jit(solution)/shard_map/while/body/eval_jaxpr/ppermute | solution.py:12
  385.5 7.9 %collective-permute-done = f32[1,256,256]{2,1,0:T(8,128)S(1)} collective-permute-done((f32[1,256,256]{2,1,0:T(8,128)S(1)}, f32[1,256,256]{2,1,0:T(8,128)S(1)}, u32[]{:S(2)}, u32[]{:S(2)}) %collective-permute-start) | collective-permute-done | bytes 262176 | tf_op jit(solution)/shard_map/while/body/eval_jaxpr/ppermute | solution.py:12
  399.1 7.9 %collective-permute-done = f32[1,256,256]{2,1,0:T(8,128)S(1)} collective-permute-done((f32[1,256,256]{2,1,0:T(8,128)S(1)}, f32[1,256,256]{2,1,0:T(8,128)S(1)}, u32[]{:S(2)}, u32[]{:S(2)}) %collective-permute-start) | collective-permute-done | bytes 262176 | tf_op jit(solution)/shard_map/while/body/eval_jaxpr/ppermute | solution.py:12
  412.7 7.9 %collective-permute-done = f32[1,256,256]{2,1,0:T(8,128)S(1)} collective-permute-done((f32[1,256,256]{2,1,0:T(8,128)S(1)}, f32[1,256,256]{2,1,0:T(8,128)S(1)}, u32[]{:S(2)}, u32[]{:S(2)}) %collective-permute-start) | collective-permute-done | bytes 262176 | tf_op jit(solution)/shard_map/while/body/eval_jaxpr/ppermute | solution.py:12
  426.2 7.9 %collective-permute-done = f32[1,256,256]{2,1,0:T(8,128)S(1)} collective-permute-done((f32[1,256,256]{2,1,0:T(8,128)S(1)}, f32[1,256,256]{2,1,0:T(8,128)S(1)}, u32[]{:S(2)}, u32[]{:S(2)}) %collective-permute-start) | collective-permute-done | bytes 262176 | tf_op jit(solution)/shard_map/while/body/eval_jaxpr/ppermute | solution.py:12
  439.8 7.9 %collective-permute-done = f32[1,256,256]{2,1,0:T(8,128)S(1)} collective-permute-done((f32[1,256,256]{2,1,0:T(8,128)S(1)}, f32[1,256,256]{2,1,0:T(8,128)S(1)}, u32[]{:S(2)}, u32[]{:S(2)}) %collective-permute-start) | collective-permute-done | bytes 262176 | tf_op jit(solution)/shard_map/while/body/eval_jaxpr/ppermute | solution.py:12
  456.1 11.2 %all-to-all-start.4 = ((bf16[16,2,2048]{2,1,0:T(2,128)(2,1)}), bf16[16,2,2048]{2,1,0:T(2,128)(2,1)S(1)}, u32[]{:S(2)}, u32[]{:S(2)}) async-start(bf16[16,2,2048]{2,1,0:T(2,128)(2,1)} %reshape.369), calls=%async_computation.4 | async-start | bytes 262144 | tf_op jit(solution)/shard_map/all_to_all | solution.py:127
  470.0 9.2 %all-to-all-done.4 = bf16[16,2,2048]{2,1,0:T(2,128)(2,1)S(1)} async-done(((bf16[16,2,2048]{2,1,0:T(2,128)(2,1)}), bf16[16,2,2048]{2,1,0:T(2,128)(2,1)S(1)}, u32[]{:S(2)}, u32[]{:S(2)}) %all-to-all-start.4) | async-done | bytes 131104 | tf_op jit(solution)/shard_map/all_to_all | solution.py:127
  484.6 10.4 %all-to-all-done.2 = bf16[16,2,2048]{2,1,0:T(2,128)(2,1)S(1)} async-done(((bf16[16,2,2048]{2,1,0:T(2,128)(2,1)}), bf16[16,2,2048]{2,1,0:T(2,128)(2,1)S(1)}, u32[]{:S(2)}, u32[]{:S(2)}) %all-to-all-start.2) | async-done | bytes 131104 | tf_op jit(solution)/shard_map/all_to_all | solution.py:126
  498.3 22.3 %psum.14 = f32[]{:T(128)} all-reduce(f32[]{:T(128)S(6)} %add.91), channel_id=1, replica_groups=mesh['seq'=32,'key'=16] {'key'}, use_global_device_ids=true, to_apply=%region_10.11 | all-reduce | flops 1 | bytes 8 | tf_op jit(solution)/shard_map/psum | solution.py:131
  520.5 85.1 %psum.15 = f32[]{:T(128)} all-reduce(f32[]{:T(128)} %psum.14), channel_id=1, replica_groups=mesh['seq'=32,'key'=16] {'seq'}, use_global_device_ids=true, to_apply=%region_11.12 | all-reduce | flops 1 | bytes 8 | tf_op jit(solution)/shard_map/psum | solution.py:132
  (356 shorter events, 376.9 us)
Async XLA Ops:
  0.7 27.9 %all-to-all-start.1 = ((bf16[256,16,16]{0,2,1:T(8,128)(2,1)}), bf16[256,16,16]{0,2,1:T(8,128)(2,1)S(1)}, u32[]{:S(2)}, u32[]{:S(2)}) async-start(bf16[256,16,16]{0,2,1:T(8,128)(2,1)} %param.15), calls=%async_computation.1 | async-start | bytes 262144 | tf_op jit(solution)/shard_map/all_to_all | solution.py:53
  28.6 17.9 %all-to-all-start.3 = ((bf16[256,16,16]{0,2,1:T(8,128)(2,1)}), bf16[256,16,16]{0,2,1:T(8,128)(2,1)S(1)}, u32[]{:S(2)}, u32[]{:S(2)}) async-start(bf16[256,16,16]{0,2,1:T(8,128)(2,1)} %param.14), calls=%async_computation.3 | async-start | bytes 262144 | tf_op jit(solution)/shard_map/all_to_all | solution.py:52
  46.5 405.4 %all-to-all-start = ((bf16[2,16,16,256]{3,2,0,1:T(8,128)(2,1)}), bf16[2,16,16,256]{3,2,0,1:T(8,128)(2,1)S(1)}, u32[]{:S(2)}, u32[]{:S(2)}) async-start(bf16[2,16,16,256]{3,2,0,1:T(8,128)(2,1)} %copy.117), calls=%async_computation | async-start | bytes 524288 | tf_op jit(solution)/shard_map/all_to_all | solution.py:54
  57.7 9.4 %collective-permute-start = (f32[1,256,256]{2,1,0:T(8,128)S(1)}, f32[1,256,256]{2,1,0:T(8,128)S(1)}, u32[]{:S(2)}, u32[]{:S(2)}) collective-permute-start(f32[1,256,256]{2,1,0:T(8,128)S(1)} %get-tuple-element.637), channel_id=1, source_target_pairs={{16,0},{32,16},{48,32},{64,48},{80,64},{96,80},{112,96},{128,112},... | collective-permute-start | bytes 786440 | tf_op jit(solution)/shard_map/while/body/eval_jaxpr/ppermute | solution.py:12
  71.0 7.7 %collective-permute-start = (f32[1,256,256]{2,1,0:T(8,128)S(1)}, f32[1,256,256]{2,1,0:T(8,128)S(1)}, u32[]{:S(2)}, u32[]{:S(2)}) collective-permute-start(f32[1,256,256]{2,1,0:T(8,128)S(1)} %get-tuple-element.637), channel_id=1, source_target_pairs={{16,0},{32,16},{48,32},{64,48},{80,64},{96,80},{112,96},{128,112},... | collective-permute-start | bytes 786440 | tf_op jit(solution)/shard_map/while/body/eval_jaxpr/ppermute | solution.py:12
  82.4 7.7 %collective-permute-start = (f32[1,256,256]{2,1,0:T(8,128)S(1)}, f32[1,256,256]{2,1,0:T(8,128)S(1)}, u32[]{:S(2)}, u32[]{:S(2)}) collective-permute-start(f32[1,256,256]{2,1,0:T(8,128)S(1)} %get-tuple-element.637), channel_id=1, source_target_pairs={{16,0},{32,16},{48,32},{64,48},{80,64},{96,80},{112,96},{128,112},... | collective-permute-start | bytes 786440 | tf_op jit(solution)/shard_map/while/body/eval_jaxpr/ppermute | solution.py:12
  105.4 7.7 %collective-permute-start = (f32[1,256,256]{2,1,0:T(8,128)S(1)}, f32[1,256,256]{2,1,0:T(8,128)S(1)}, u32[]{:S(2)}, u32[]{:S(2)}) collective-permute-start(f32[1,256,256]{2,1,0:T(8,128)S(1)} %get-tuple-element.637), channel_id=1, source_target_pairs={{16,0},{32,16},{48,32},{64,48},{80,64},{96,80},{112,96},{128,112},... | collective-permute-start | bytes 786440 | tf_op jit(solution)/shard_map/while/body/eval_jaxpr/ppermute | solution.py:12
  116.8 7.7 %collective-permute-start = (f32[1,256,256]{2,1,0:T(8,128)S(1)}, f32[1,256,256]{2,1,0:T(8,128)S(1)}, u32[]{:S(2)}, u32[]{:S(2)}) collective-permute-start(f32[1,256,256]{2,1,0:T(8,128)S(1)} %get-tuple-element.637), channel_id=1, source_target_pairs={{16,0},{32,16},{48,32},{64,48},{80,64},{96,80},{112,96},{128,112},... | collective-permute-start | bytes 786440 | tf_op jit(solution)/shard_map/while/body/eval_jaxpr/ppermute | solution.py:12
  139.7 7.7 %collective-permute-start = (f32[1,256,256]{2,1,0:T(8,128)S(1)}, f32[1,256,256]{2,1,0:T(8,128)S(1)}, u32[]{:S(2)}, u32[]{:S(2)}) collective-permute-start(f32[1,256,256]{2,1,0:T(8,128)S(1)} %get-tuple-element.637), channel_id=1, source_target_pairs={{16,0},{32,16},{48,32},{64,48},{80,64},{96,80},{112,96},{128,112},... | collective-permute-start | bytes 786440 | tf_op jit(solution)/shard_map/while/body/eval_jaxpr/ppermute | solution.py:12
  151.2 7.7 %collective-permute-start = (f32[1,256,256]{2,1,0:T(8,128)S(1)}, f32[1,256,256]{2,1,0:T(8,128)S(1)}, u32[]{:S(2)}, u32[]{:S(2)}) collective-permute-start(f32[1,256,256]{2,1,0:T(8,128)S(1)} %get-tuple-element.637), channel_id=1, source_target_pairs={{16,0},{32,16},{48,32},{64,48},{80,64},{96,80},{112,96},{128,112},... | collective-permute-start | bytes 786440 | tf_op jit(solution)/shard_map/while/body/eval_jaxpr/ppermute | solution.py:12
  174.1 7.7 %collective-permute-start = (f32[1,256,256]{2,1,0:T(8,128)S(1)}, f32[1,256,256]{2,1,0:T(8,128)S(1)}, u32[]{:S(2)}, u32[]{:S(2)}) collective-permute-start(f32[1,256,256]{2,1,0:T(8,128)S(1)} %get-tuple-element.637), channel_id=1, source_target_pairs={{16,0},{32,16},{48,32},{64,48},{80,64},{96,80},{112,96},{128,112},... | collective-permute-start | bytes 786440 | tf_op jit(solution)/shard_map/while/body/eval_jaxpr/ppermute | solution.py:12
  185.6 7.7 %collective-permute-start = (f32[1,256,256]{2,1,0:T(8,128)S(1)}, f32[1,256,256]{2,1,0:T(8,128)S(1)}, u32[]{:S(2)}, u32[]{:S(2)}) collective-permute-start(f32[1,256,256]{2,1,0:T(8,128)S(1)} %get-tuple-element.637), channel_id=1, source_target_pairs={{16,0},{32,16},{48,32},{64,48},{80,64},{96,80},{112,96},{128,112},... | collective-permute-start | bytes 786440 | tf_op jit(solution)/shard_map/while/body/eval_jaxpr/ppermute | solution.py:12
  208.5 8.4 %collective-permute-start = (f32[1,256,256]{2,1,0:T(8,128)S(1)}, f32[1,256,256]{2,1,0:T(8,128)S(1)}, u32[]{:S(2)}, u32[]{:S(2)}) collective-permute-start(f32[1,256,256]{2,1,0:T(8,128)S(1)} %get-tuple-element.637), channel_id=1, source_target_pairs={{16,0},{32,16},{48,32},{64,48},{80,64},{96,80},{112,96},{128,112},... | collective-permute-start | bytes 786440 | tf_op jit(solution)/shard_map/while/body/eval_jaxpr/ppermute | solution.py:12
  220.7 9.8 %collective-permute-start = (f32[1,256,256]{2,1,0:T(8,128)S(1)}, f32[1,256,256]{2,1,0:T(8,128)S(1)}, u32[]{:S(2)}, u32[]{:S(2)}) collective-permute-start(f32[1,256,256]{2,1,0:T(8,128)S(1)} %get-tuple-element.637), channel_id=1, source_target_pairs={{16,0},{32,16},{48,32},{64,48},{80,64},{96,80},{112,96},{128,112},... | collective-permute-start | bytes 786440 | tf_op jit(solution)/shard_map/while/body/eval_jaxpr/ppermute | solution.py:12
  234.3 9.8 %collective-permute-start = (f32[1,256,256]{2,1,0:T(8,128)S(1)}, f32[1,256,256]{2,1,0:T(8,128)S(1)}, u32[]{:S(2)}, u32[]{:S(2)}) collective-permute-start(f32[1,256,256]{2,1,0:T(8,128)S(1)} %get-tuple-element.637), channel_id=1, source_target_pairs={{16,0},{32,16},{48,32},{64,48},{80,64},{96,80},{112,96},{128,112},... | collective-permute-start | bytes 786440 | tf_op jit(solution)/shard_map/while/body/eval_jaxpr/ppermute | solution.py:12
  247.9 9.8 %collective-permute-start = (f32[1,256,256]{2,1,0:T(8,128)S(1)}, f32[1,256,256]{2,1,0:T(8,128)S(1)}, u32[]{:S(2)}, u32[]{:S(2)}) collective-permute-start(f32[1,256,256]{2,1,0:T(8,128)S(1)} %get-tuple-element.637), channel_id=1, source_target_pairs={{16,0},{32,16},{48,32},{64,48},{80,64},{96,80},{112,96},{128,112},... | collective-permute-start | bytes 786440 | tf_op jit(solution)/shard_map/while/body/eval_jaxpr/ppermute | solution.py:12
  261.4 9.8 %collective-permute-start = (f32[1,256,256]{2,1,0:T(8,128)S(1)}, f32[1,256,256]{2,1,0:T(8,128)S(1)}, u32[]{:S(2)}, u32[]{:S(2)}) collective-permute-start(f32[1,256,256]{2,1,0:T(8,128)S(1)} %get-tuple-element.637), channel_id=1, source_target_pairs={{16,0},{32,16},{48,32},{64,48},{80,64},{96,80},{112,96},{128,112},... | collective-permute-start | bytes 786440 | tf_op jit(solution)/shard_map/while/body/eval_jaxpr/ppermute | solution.py:12
  275.0 9.8 %collective-permute-start = (f32[1,256,256]{2,1,0:T(8,128)S(1)}, f32[1,256,256]{2,1,0:T(8,128)S(1)}, u32[]{:S(2)}, u32[]{:S(2)}) collective-permute-start(f32[1,256,256]{2,1,0:T(8,128)S(1)} %get-tuple-element.637), channel_id=1, source_target_pairs={{16,0},{32,16},{48,32},{64,48},{80,64},{96,80},{112,96},{128,112},... | collective-permute-start | bytes 786440 | tf_op jit(solution)/shard_map/while/body/eval_jaxpr/ppermute | solution.py:12
  288.6 9.8 %collective-permute-start = (f32[1,256,256]{2,1,0:T(8,128)S(1)}, f32[1,256,256]{2,1,0:T(8,128)S(1)}, u32[]{:S(2)}, u32[]{:S(2)}) collective-permute-start(f32[1,256,256]{2,1,0:T(8,128)S(1)} %get-tuple-element.637), channel_id=1, source_target_pairs={{16,0},{32,16},{48,32},{64,48},{80,64},{96,80},{112,96},{128,112},... | collective-permute-start | bytes 786440 | tf_op jit(solution)/shard_map/while/body/eval_jaxpr/ppermute | solution.py:12
  302.2 9.8 %collective-permute-start = (f32[1,256,256]{2,1,0:T(8,128)S(1)}, f32[1,256,256]{2,1,0:T(8,128)S(1)}, u32[]{:S(2)}, u32[]{:S(2)}) collective-permute-start(f32[1,256,256]{2,1,0:T(8,128)S(1)} %get-tuple-element.637), channel_id=1, source_target_pairs={{16,0},{32,16},{48,32},{64,48},{80,64},{96,80},{112,96},{128,112},... | collective-permute-start | bytes 786440 | tf_op jit(solution)/shard_map/while/body/eval_jaxpr/ppermute | solution.py:12
  315.7 9.8 %collective-permute-start = (f32[1,256,256]{2,1,0:T(8,128)S(1)}, f32[1,256,256]{2,1,0:T(8,128)S(1)}, u32[]{:S(2)}, u32[]{:S(2)}) collective-permute-start(f32[1,256,256]{2,1,0:T(8,128)S(1)} %get-tuple-element.637), channel_id=1, source_target_pairs={{16,0},{32,16},{48,32},{64,48},{80,64},{96,80},{112,96},{128,112},... | collective-permute-start | bytes 786440 | tf_op jit(solution)/shard_map/while/body/eval_jaxpr/ppermute | solution.py:12
  329.3 9.8 %collective-permute-start = (f32[1,256,256]{2,1,0:T(8,128)S(1)}, f32[1,256,256]{2,1,0:T(8,128)S(1)}, u32[]{:S(2)}, u32[]{:S(2)}) collective-permute-start(f32[1,256,256]{2,1,0:T(8,128)S(1)} %get-tuple-element.637), channel_id=1, source_target_pairs={{16,0},{32,16},{48,32},{64,48},{80,64},{96,80},{112,96},{128,112},... | collective-permute-start | bytes 786440 | tf_op jit(solution)/shard_map/while/body/eval_jaxpr/ppermute | solution.py:12
  342.9 9.8 %collective-permute-start = (f32[1,256,256]{2,1,0:T(8,128)S(1)}, f32[1,256,256]{2,1,0:T(8,128)S(1)}, u32[]{:S(2)}, u32[]{:S(2)}) collective-permute-start(f32[1,256,256]{2,1,0:T(8,128)S(1)} %get-tuple-element.637), channel_id=1, source_target_pairs={{16,0},{32,16},{48,32},{64,48},{80,64},{96,80},{112,96},{128,112},... | collective-permute-start | bytes 786440 | tf_op jit(solution)/shard_map/while/body/eval_jaxpr/ppermute | solution.py:12
  356.4 9.8 %collective-permute-start = (f32[1,256,256]{2,1,0:T(8,128)S(1)}, f32[1,256,256]{2,1,0:T(8,128)S(1)}, u32[]{:S(2)}, u32[]{:S(2)}) collective-permute-start(f32[1,256,256]{2,1,0:T(8,128)S(1)} %get-tuple-element.637), channel_id=1, source_target_pairs={{16,0},{32,16},{48,32},{64,48},{80,64},{96,80},{112,96},{128,112},... | collective-permute-start | bytes 786440 | tf_op jit(solution)/shard_map/while/body/eval_jaxpr/ppermute | solution.py:12
  370.0 9.8 %collective-permute-start = (f32[1,256,256]{2,1,0:T(8,128)S(1)}, f32[1,256,256]{2,1,0:T(8,128)S(1)}, u32[]{:S(2)}, u32[]{:S(2)}) collective-permute-start(f32[1,256,256]{2,1,0:T(8,128)S(1)} %get-tuple-element.637), channel_id=1, source_target_pairs={{16,0},{32,16},{48,32},{64,48},{80,64},{96,80},{112,96},{128,112},... | collective-permute-start | bytes 786440 | tf_op jit(solution)/shard_map/while/body/eval_jaxpr/ppermute | solution.py:12
  383.6 9.8 %collective-permute-start = (f32[1,256,256]{2,1,0:T(8,128)S(1)}, f32[1,256,256]{2,1,0:T(8,128)S(1)}, u32[]{:S(2)}, u32[]{:S(2)}) collective-permute-start(f32[1,256,256]{2,1,0:T(8,128)S(1)} %get-tuple-element.637), channel_id=1, source_target_pairs={{16,0},{32,16},{48,32},{64,48},{80,64},{96,80},{112,96},{128,112},... | collective-permute-start | bytes 786440 | tf_op jit(solution)/shard_map/while/body/eval_jaxpr/ppermute | solution.py:12
  397.2 9.8 %collective-permute-start = (f32[1,256,256]{2,1,0:T(8,128)S(1)}, f32[1,256,256]{2,1,0:T(8,128)S(1)}, u32[]{:S(2)}, u32[]{:S(2)}) collective-permute-start(f32[1,256,256]{2,1,0:T(8,128)S(1)} %get-tuple-element.637), channel_id=1, source_target_pairs={{16,0},{32,16},{48,32},{64,48},{80,64},{96,80},{112,96},{128,112},... | collective-permute-start | bytes 786440 | tf_op jit(solution)/shard_map/while/body/eval_jaxpr/ppermute | solution.py:12
  410.7 9.8 %collective-permute-start = (f32[1,256,256]{2,1,0:T(8,128)S(1)}, f32[1,256,256]{2,1,0:T(8,128)S(1)}, u32[]{:S(2)}, u32[]{:S(2)}) collective-permute-start(f32[1,256,256]{2,1,0:T(8,128)S(1)} %get-tuple-element.637), channel_id=1, source_target_pairs={{16,0},{32,16},{48,32},{64,48},{80,64},{96,80},{112,96},{128,112},... | collective-permute-start | bytes 786440 | tf_op jit(solution)/shard_map/while/body/eval_jaxpr/ppermute | solution.py:12
  424.3 9.8 %collective-permute-start = (f32[1,256,256]{2,1,0:T(8,128)S(1)}, f32[1,256,256]{2,1,0:T(8,128)S(1)}, u32[]{:S(2)}, u32[]{:S(2)}) collective-permute-start(f32[1,256,256]{2,1,0:T(8,128)S(1)} %get-tuple-element.637), channel_id=1, source_target_pairs={{16,0},{32,16},{48,32},{64,48},{80,64},{96,80},{112,96},{128,112},... | collective-permute-start | bytes 786440 | tf_op jit(solution)/shard_map/while/body/eval_jaxpr/ppermute | solution.py:12
  437.9 9.8 %collective-permute-start = (f32[1,256,256]{2,1,0:T(8,128)S(1)}, f32[1,256,256]{2,1,0:T(8,128)S(1)}, u32[]{:S(2)}, u32[]{:S(2)}) collective-permute-start(f32[1,256,256]{2,1,0:T(8,128)S(1)} %get-tuple-element.637), channel_id=1, source_target_pairs={{16,0},{32,16},{48,32},{64,48},{80,64},{96,80},{112,96},{128,112},... | collective-permute-start | bytes 786440 | tf_op jit(solution)/shard_map/while/body/eval_jaxpr/ppermute | solution.py:12
  456.1 23.1 %all-to-all-start.4 = ((bf16[16,2,2048]{2,1,0:T(2,128)(2,1)}), bf16[16,2,2048]{2,1,0:T(2,128)(2,1)S(1)}, u32[]{:S(2)}, u32[]{:S(2)}) async-start(bf16[16,2,2048]{2,1,0:T(2,128)(2,1)} %reshape.369), calls=%async_computation.4 | async-start | bytes 262144 | tf_op jit(solution)/shard_map/all_to_all | solution.py:127
  479.2 15.8 %all-to-all-start.2 = ((bf16[16,2,2048]{2,1,0:T(2,128)(2,1)}), bf16[16,2,2048]{2,1,0:T(2,128)(2,1)S(1)}, u32[]{:S(2)}, u32[]{:S(2)}) async-start(bf16[16,2,2048]{2,1,0:T(2,128)(2,1)} %reshape.367), calls=%async_computation.2 | async-start | bytes 262144 | tf_op jit(solution)/shard_map/all_to_all | solution.py:126
  (10 other events, 119.9 us)
